TPU v7x, 128 devices: a whole 4x4x4 slice. The times are simulated.
128 devices in a mesh: lon: 16 (over y, x_hi, core), lat: 8 (over x_lo, z).
Axes of the slice: x: 4 (x_hi: 2, x_lo: 2; x = x_hi * 2 + x_lo), y: 4, z: 4, core: 2. Of those that a mesh axis runs over, the one named last changes fastest.
Arguments:
- tracers: float32 [6, 24, 512, 2048], P(None, None, 'lat', 'lon'), may hold values from -6 to 6
- flow_east: float32 [24, 512, 2048], P(None, 'lat', 'lon'), may hold values from -0.35 to 0.35
- flow_north: float32 [24, 512, 2048], P(None, 'lat', 'lon'), may hold values from -0.35 to 0.35
- sea_mask: int32 [24, 512, 2048], P(None, 'lat', 'lon'), may hold values 0 or 1
- atm_fields: bfloat16 [4, 1048576], P(None, ('lon', 'lat')), may hold values from -6 to 6
- remap_weights: bfloat16 [32768, 128, 128], P(('lon', 'lat')), may hold values from -0.5 to 0.5
- remap_src: int32 [32768], P(('lon', 'lat')), may hold values from 0 to 63
- remap_dst: int32 [32768], P(('lon', 'lat')), may hold values from 0 to 8191, as said below
- fold_partner: int32 [2048], P('lon'), may hold values from 0 to 2047, as said below
Outputs:
- forcing: float32 [4, 512, 2048], P(None, 'lat', 'lon')
- tracers_next: float32 [6, 24, 512, 2048], P(None, None, 'lat', 'lon')
Inputs may be any that keep to these rules, and one draw needn't show every extreme that they name: `remap_dst`: the weight blocks held by one device name at most 4 destination blocks on any one device; in every draw one device is named 4 times by the blocks of every device. fold_partner[i] = (c - i) mod 2048 for one c.
All inputs are finite; a program needn't handle non-finite values. No bound on the sum of `sea_mask` on one device may be relied on, other than what follows from the above.
Results may differ from a plain program's by a relative error of at most 0.0003.
Values sent between devices are 32-bit elements; how exact they have to be, the bound alone decides.
No kernel may reach another device: no remote copies, remote signals or barrier semaphores. Data moves between devices by JAX's collectives and lax.ppermute only.
A program may use at most 192 MiB of HBM per device.

v0:
```python
import functools

import jax
import jax.numpy as jnp
from jax import lax
from jax.experimental import pallas as pl
from jax.experimental.pallas import tpu as pltpu
from jax.sharding import PartitionSpec as P

HEAT_SCALE = 0.1
FRESH_SCALE = 0.03
STRESS_SCALE = 0.02
HEAT_ALPHA_COEFF = 0.2
SALT_BETA_COEFF = 0.8
SLOPE_EPS = 0.5
DIFFUSIVITY = 0.1

NTR = 6
ROWS = 64
LANES = 128
GROUPS = 7
LABEL_LANE = 32
F32 = jnp.float32
TOGETHER = 2
EDGE_LEVELS = 8
VMEM_LIMIT = 56 * 1024 * 1024


def roll(x, shift):
    return pltpu.roll(x, shift % LANES, axis=1)


def lanes_of(shape):
    return lax.broadcasted_iota(jnp.int32, shape, len(shape) - 1)


def pack_kernel(
    tracers, east, north, mask, both_out, cols_out, up_out, down_out,
    cells, flows_e, flows_n, lands, both_ref, cols_ref, up_ref, down_ref, in_sem, out_sem
):
    lane_group = lanes_of((8, LANES)) // 4
    levels = east.shape[0]
    step = 4
    chunks = levels // step

    def in_copies(i):
        part = pl.ds(i * step, step)
        pairs = ((east, flows_e), (north, flows_n), (mask, lands))
        copies = [pltpu.make_async_copy(a.at[part], b.at[part], in_sem.at[j, i]) for j, (a, b) in enumerate(pairs)]
        return copies + [pltpu.make_async_copy(tracers.at[:, part], cells.at[:, part], in_sem.at[3, i])]

    def out_copies(i):
        part = pl.ds(i * step, step)
        pairs = ((both_ref, both_out), (cols_ref, cols_out), (up_ref, up_out), (down_ref, down_out))
        return [pltpu.make_async_copy(a.at[part], b.at[part], out_sem.at[j, i]) for j, (a, b) in enumerate(pairs)]

    for i in range(chunks):
        for copy in in_copies(i):
            copy.start()

    def chunk(i, _):
        for copy in in_copies(i):
            copy.wait()
        for j in range(step):
            one(i * step + j)
        for copy in out_copies(i):
            copy.start()
        return 0

    def one(k):
        land = lands[k].astype(F32)
        for h in range(2):
            total = jnp.zeros((8, LANES), F32)
            for rr in range(4):
                start = (4 * h + rr) * 8
                for f in range(8):
                    if f < NTR:
                        tile = cells[f, k, start : start + 8]
                    else:
                        tile = land[start : start + 8] if f == 7 else flows_e[k, start : start + 8]
                    moved = roll(tile, 2 + 32 * rr + 4 * f)
                    total = jnp.where(lane_group == 8 * rr + f, moved, total)
            both_ref[k, h] = total
            cols_ref[k, h] = total

        def row(f, r):
            if f < NTR:
                return cells[f, k, r : r + 1]
            return land[r : r + 1] if f == 7 else flows_n[k, r : r + 1]

        for f in range(8):
            last = row(f, ROWS - 1)
            both_ref[k, 2, f : f + 1] = last
            up_ref[k, 0, f : f + 1] = row(f, ROWS - 2)
            up_ref[k, 1, f : f + 1] = last
            for i in range(2):
                down_ref[k, i, f : f + 1] = row(f, i)

    lax.fori_loop(0, chunks, chunk, 0)
    for i in range(chunks):
        for copy in out_copies(i):
            copy.wait()


def pack_halos(tracers, east, north, mask):
    levels = east.shape[0]
    sizes = [(levels, n, 8, LANES) for n in (3, 2, 2, 2)]
    flow = (levels, ROWS, LANES)
    return pl.pallas_call(
        pack_kernel,
        in_specs=[pl.BlockSpec(memory_space=pltpu.HBM)] * 4,
        out_specs=[pl.BlockSpec(memory_space=pl.ANY)] * 4,
        out_shape=[jax.ShapeDtypeStruct(x, F32) for x in sizes],
        scratch_shapes=[
            pltpu.VMEM(tracers.shape, F32),
            pltpu.VMEM(flow, F32),
            pltpu.VMEM(flow, F32),
            pltpu.VMEM(flow, jnp.int32),
        ]
        + [pltpu.VMEM(x, F32) for x in sizes]
        + [pltpu.SemaphoreType.DMA((4, 6)), pltpu.SemaphoreType.DMA((4, 6))],
        compiler_params=pltpu.CompilerParams(vmem_limit_bytes=VMEM_LIMIT),
        name="pack_halos",
    )(tracers, east, north, mask)


def remap_kernel(n_lon, n_lat, src, dst, fold, atm, weights_hbm, out, weights, blocks, edge, labels, count, weight_sem):
    devices = n_lon * n_lat
    sends = weights.shape[0]
    chunks = weight_sem.shape[0]
    per_chunk = sends // chunks

    def weight_copy(i):
        part = pl.ds(i * per_chunk, per_chunk)
        return pltpu.make_async_copy(weights_hbm.at[part], weights.at[part], weight_sem.at[i])

    for i in range(chunks):
        weight_copy(i).start()
    wide = atm[...].astype(F32)
    for b in range(blocks.shape[0]):
        blocks[b, 0:4] = wide[:, b * LANES : (b + 1) * LANES]
    out[...] = jnp.zeros_like(out)
    edge[...] = jnp.zeros_like(edge)
    labels[...] = jnp.zeros_like(labels)

    def clear(i, _):
        count[i] = 0
        return 0

    lax.fori_loop(0, devices, clear, 0, unroll=8)

    lane1 = lanes_of((1, LANES))
    batch = 8

    per = per_chunk // batch

    def chunk(i, _):
        weight_copy(i).wait()
        lax.fori_loop(0, per, lambda j, x: several(i * per + j, x), 0, unroll=per)
        return 0

    def several(i, _):
        places, lefts = [], []
        for j in range(batch):
            w = batch * i + j
            place = dst[w]
            lon = place & (n_lon - 1) if n_lon & (n_lon - 1) == 0 else place % n_lon
            row = place // n_lon
            local = row % ROWS
            owner = lon * n_lat + row // ROWS
            slot = count[owner]
            count[owner] = slot + 1
            kind = jnp.where(local < 2, local, local - (ROWS - 4))
            is_edge = jnp.logical_or(local < 2, local >= ROWS - 2)
            places.append((owner, slot, local, jnp.where(is_edge, owner * 4 + kind, devices * 4)))
            lefts.append(blocks[src[w], 0:4])
        left = jnp.concatenate(lefts, 0).astype(jnp.bfloat16)
        right = weights[pl.ds(pl.multiple_of(batch * i, batch), batch)].reshape(batch * LANES, LANES)
        products = lax.dot_general(left, right, (((1,), (1,)), ((), ())), preferred_element_type=F32)
        for j, (owner, slot, local, at) in enumerate(places):
            product = products[4 * j : 4 * j + 4, LANES * j : LANES * (j + 1)]
            out[owner * GROUPS + slot] = product
            labels[pl.ds(owner, 1)] = jnp.where(lane1 == slot, (local + 1).astype(F32), labels[pl.ds(owner, 1)])
            edge[at] = edge[at] + product
        return 0

    lax.fori_loop(0, chunks, chunk, 0)

    lane4 = lanes_of((4, LANES))
    high = fold[0] // LANES
    low = fold[0] % LANES
    strips = []
    for p in range(n_lon):
        first = edge[(((high - p + 2 * n_lon) % n_lon) * n_lat + n_lat - 1) * 4 + 3]
        second = edge[(((high - p - 1 + 2 * n_lon) % n_lon) * n_lat + n_lat - 1) * 4 + 3]
        strips.append(jnp.where(lane4 <= low, first, second))
    ghost = reversed_lanes(jnp.concatenate(strips, 0), low)
    for owner in range(devices):
        total = jnp.zeros((4, LANES), F32)
        for n in range(4):
            moved = roll(out[owner * GROUPS + n], 2 + 4 * n)
            total = jnp.where(lane4 // 4 == n, moved, total)
        out[owner * GROUPS + 4] = total
    own = labels[...]
    lane = lanes_of(own.shape) - LABEL_LANE
    west = jnp.concatenate([own[devices - n_lat :], own[: devices - n_lat]], 0)
    east = jnp.concatenate([own[n_lat:], own[:n_lat]], 0)
    labels[...] = jnp.where(
        lane < 4, roll(own, LABEL_LANE), jnp.where(lane < 8, roll(west, LABEL_LANE + 4), roll(east, LABEL_LANE + 8))
    )
    for lat in range(n_lat):
        packs = [out[(lon * n_lat + lat) * GROUPS + 4] for lon in range(n_lon)]
        for lon in range(n_lon):
            owner = lon * n_lat + lat
            base = owner * GROUPS
            beside = jnp.where(lane4 < 16, packs[(lon - 1) % n_lon], roll(packs[(lon + 1) % n_lon], 16))
            out[base + 4, 0:3] = beside[0:3]
            out[base + 4, 0:1] = beside[0:1] + labels[owner : owner + 1]
            if lat < n_lat - 1:
                above = (owner + 1) * 4
                out[base + 5, 0:2] = edge[above, 0:2]
                out[base + 5, 2:4] = edge[above + 1, 0:2]
            else:
                out[base + 5, 0:2] = ghost[4 * lon : 4 * lon + 2]
                out[base + 5, 2:4] = ghost[4 * lon : 4 * lon + 2]
            if lat > 0:
                below = (owner - 1) * 4
                out[base + 6, 0:2] = edge[below + 3, 0:2]
                out[base + 6, 2:4] = edge[below + 2, 0:2]
                out[base + 4, 3:4] = edge[below + 3, 3:4]
            else:
                out[base + 4, 3:4] = jnp.zeros((1, LANES), F32)


def reversed_lanes(x, low):
    before = lax.broadcasted_iota(jnp.int32, (LANES, LANES), 0)
    after = lax.broadcasted_iota(jnp.int32, (LANES, LANES), 1)
    table = (before == (low - after + LANES) % LANES).astype(F32)
    return jnp.dot(x, table, precision=lax.Precision.HIGHEST, preferred_element_type=F32)


def remap(atm, weights, src, dst, fold_c, n_lon, n_lat):
    devices = n_lon * n_lat
    blocks = atm.shape[1] // LANES
    smem = pl.BlockSpec(memory_space=pltpu.SMEM)
    return pl.pallas_call(
        functools.partial(remap_kernel, n_lon, n_lat),
        in_specs=[smem, smem, smem, pl.BlockSpec(memory_space=pltpu.VMEM), pl.BlockSpec(memory_space=pltpu.HBM)],
        out_specs=pl.BlockSpec(memory_space=pltpu.VMEM),
        out_shape=jax.ShapeDtypeStruct((devices * GROUPS, 4, LANES), F32),
        scratch_shapes=[
            pltpu.VMEM(weights.shape, weights.dtype),
            pltpu.VMEM((blocks, 8, LANES), F32),
            pltpu.VMEM((devices * 4 + 1, 4, LANES), F32),
            pltpu.VMEM((devices, LANES), F32),
            pltpu.SMEM((devices,), jnp.int32),
            pltpu.SemaphoreType.DMA((8,)),
        ],
        compiler_params=pltpu.CompilerParams(vmem_limit_bytes=VMEM_LIMIT),
        name="remap",
    )(src, dst, fold_c, atm, weights)


def minmod(a, b):
    return jnp.maximum(jnp.minimum(a, b), jnp.minimum(jnp.maximum(a, b), 0.0))


def face_coefficients(flow, mask, drho, zrho):
    diff = DIFFUSIVITY * mask
    strat = 0.25 * zrho
    slope = drho * strat / (strat * strat + SLOPE_EPS)
    up = jnp.maximum(flow, 0.0)
    down = jnp.minimum(flow, 0.0)
    return (
        up + diff,
        down - diff,
        0.5 * up * (1.0 - up),
        -0.5 * down * (1.0 + down),
        0.25 * diff * slope,
    )


def density(temperature, salinity):
    return SALT_BETA_COEFF * salinity - HEAT_ALPHA_COEFF * temperature


def spread(x, lane32):
    for width in (4, 8, 16):
        x = jnp.where(lane32 < width, x, roll(x, width))
    return x


def edge_values(halo, own):
    lane = lanes_of(halo(0, 0).shape)
    lane4, lane32 = lane % 4, lane % 32
    east = lane4 == 0
    parts = []
    for h in range(2):
        p, o = halo(0, h), own(0, h)
        zp, zo = halo(1, h) - halo(-1, h), own(1, h) - own(-1, h)
        o1, p2, zp2 = roll(o, -1), roll(p, -2), roll(zp, -2)
        zo1 = roll(zo, -1)
        parts.append(
            (
                jnp.where(east, o, roll(p, 1)),
                jnp.where(east, o1, p),
                jnp.where(east, p2, o1),
                jnp.where(east, roll(p, -3), roll(o, -2)),
                jnp.where(east, zo1, zp),
                jnp.where(east, zp2, zo1),
            )
        )
    c0, c1, c2, c3, z1, z2 = [jnp.where(lane4 < 2, x, roll(y, 2)) for x, y in zip(*parts)]
    d2 = c2 - c1
    s1, s2 = minmod(d2, c1 - c0), minmod(c3 - c2, d2)
    z = z1 + z2
    mask = roll(c1 * c2, -28)
    coefs = face_coefficients(roll(c1, -24) * mask, mask, density(d2, roll(d2, -4)), density(z, roll(z, -4)))
    a, b, p, q, v = [spread(x, lane32) for x in coefs]
    return jnp.where(lane4 % 2 == 0, s1, s2), a * c1 + b * c2 + p * s1 + q * s2 + v * z


def in_step(*levels):
    levels = list(levels)
    while levels:
        levels = [level for level in levels if next(level, None) is not None]


def level_step(below, cpad, above, rows_below, rows_above, edge_slope, edge_flux, east, north, land, write, scratch):
    zpad, hpad, gpad, slope, xco, yco, mpad, tops = scratch
    lane = lanes_of((8, LANES))
    first_lane, last_lane = lane == 0, lane == LANES - 1
    mid = slice(8, 72)

    below1, below2 = rows_below(0, 1), rows_below(0, 0)
    above1, above2 = rows_above(0, 0), rows_above(0, 1)
    z_below = rows_below(1, 1) - rows_below(-1, 1)
    z_above = rows_above(1, 0) - rows_above(-1, 0)
    for t in range(NTR):
        zpad[t, mid] = above[t, mid] - below[t, mid]
        cpad[t, 7:8] = below1[t : t + 1]
        cpad[t, 72:73] = above1[t : t + 1]
        tops[0, t : t + 1] = cpad[t, 8:9]
        tops[1, t : t + 1] = cpad[t, 71:72]
    for t in range(2):
        zpad[t, 72:73] = z_above[t : t + 1]
    tops[2] = zpad[0, 8:16]
    tops[3] = zpad[1, 8:16]
    mpad[mid] = land
    mpad[72:73] = above1[7:8]

    yield True

    def at_edge(x, r, f):
        return roll(x, -(32 * (r % 4) + 4 * f + 2 * (r // 4) + 1))

    def x_face(t):
        c, z = cpad[t, mid], zpad[t, mid]
        return roll(c, -1) - c, z + roll(z, -1)

    (dt, zt), (ds, zs) = x_face(0), x_face(1)
    mask = land * roll(land, -1)
    a, b, p, q, v = face_coefficients(east * mask, mask, density(dt, ds), density(zt, zs))
    for i, x in enumerate((a, p, v, roll(b, 1), roll(q, 1), roll(v, 1))):
        xco[i] = x
    yield True

    def y_face(t):
        return cpad[t, 9:73] - cpad[t, mid], zpad[t, mid] + zpad[t, 9:73]

    (dt, zt), (ds, zs) = y_face(0), y_face(1)
    mask = land * mpad[9:73]
    for i, x in enumerate(face_coefficients(north * mask, mask, density(dt, ds), density(zt, zs))):
        yco[i, mid] = x
    row0 = tops[0]
    mask = below1[7:8] * mpad[8:9]
    d = row0 - below1
    a, b, p, q, v = face_coefficients(
        below1[6:7] * mask,
        mask,
        density(d[0:1], d[1:2]),
        density(z_below[0:1] + tops[2, 0:1], z_below[1:2] + tops[3, 0:1]),
    )
    yco[1, 7:8], yco[3, 7:8], yco[4, 7:8] = b, q, v
    h_below = a * below1 + p * minmod(d, below1 - below2) + v * z_below
    b, q, v = yco[1, 71:72], yco[3, 71:72], yco[4, 71:72]
    g_above = b * above1 + q * minmod(above2 - above1, above1 - tops[1]) + v * z_above
    for t in range(NTR):
        hpad[t, 7:8] = h_below[t : t + 1]
        gpad[t, 72:73] = g_above[t : t + 1]

    yield True
    at_side = jnp.logical_or(first_lane, last_lane)
    for r in range(8):
        here = slice(8 + 8 * r, 16 + 8 * r)
        lower, upper = slice(7 + 8 * r, 15 + 8 * r), slice(9 + 8 * r, 17 + 8 * r)
        ya, yp, yv, yb, yq, yw = yco[0, here], yco[2, here], yco[4, here], yco[1, lower], yco[3, lower], yco[4, lower]
        for t in range(NTR):
            c, z = cpad[t, here], zpad[t, here]
            s = minmod(roll(c, -1) - c, c - roll(c, 1))
            slope[t, 8 * r : 8 * r + 8] = jnp.where(at_side, at_edge(edge_slope, r, t), s)
            s = minmod(cpad[t, upper] - c, c - cpad[t, lower])
            hpad[t, here] = ya * c + yp * s + yv * z
            gpad[t, here] = yb * c + yq * s + yw * z
        yield True
    for r in range(8):
        here = slice(8 + 8 * r, 16 + 8 * r)
        lower, upper = slice(7 + 8 * r, 15 + 8 * r), slice(9 + 8 * r, 17 + 8 * r)
        part = slice(8 * r, 8 * r + 8)
        xa, xp, xv, xb, xq, xw = [xco[i, part] for i in range(6)]
        wet = mpad[here]
        for t in range(NTR):
            c, z, s = cpad[t, here], zpad[t, here], slope[t, part]
            h = xa * c + xp * s + xv * z
            g = xb * c + xq * s + xw * z
            flux = at_edge(edge_flux, r, t)
            out_east = jnp.where(last_lane, flux, h + roll(g, -1))
            in_west = jnp.where(first_lane, flux, g + roll(h, 1))
            out_north = hpad[t, here] + gpad[t, upper]
            in_south = hpad[t, lower] + gpad[t, here]
            write(t, part, wet * (c - (out_east - in_west) - (out_north - in_south)))
        yield True


def level_scratch():
    padded = pltpu.VMEM((NTR, 80, LANES), F32)
    return [
        padded,
        padded,
        padded,
        pltpu.VMEM((NTR, ROWS, LANES), F32),
        pltpu.VMEM((6, ROWS, LANES), F32),
        pltpu.VMEM((5, 80, LANES), F32),
        pltpu.VMEM((80, LANES), F32),
        pltpu.VMEM((4, 8, LANES), F32),
    ]


def chunk_spans(lo, hi):
    spans, size = [], 4
    while lo < hi:
        end = min(lo + size, hi)
        if hi - end < size:
            end = hi
        spans.append((lo, end))
        lo, size = end, size + 2
    return spans


def deep_kernel(
    first, together, top, tracers, east, north, mask, west_cols, east_cols, own_cols, row_below, row_above, ghost, out,
    cells, flows_e, flows_n, lands, west_v, east_v, own_v, below_v, above_v, ghost_v, results, edges, halo_sem, level_sem, out_sem, *scratch
):
    levels = cells.shape[1]

    def halo_copies():
        pairs = ((row_below, below_v), (row_above, above_v), (west_cols, west_v), (east_cols, east_v), (own_cols, own_v), (ghost, ghost_v))
        return [pltpu.make_async_copy(a, b, halo_sem.at[i]) for i, (a, b) in enumerate(pairs)]

    spans = chunk_spans(first - 1, levels)
    sends = chunk_spans(first, levels)[::-1]
    sends = [(first + levels - hi, first + levels - lo) for lo, hi in sends]

    def cell_copy(i):
        lo, hi = spans[i]
        return pltpu.make_async_copy(tracers.at[:, lo:hi], cells.at[:, lo:hi, 8:72], level_sem.at[0, i])

    def flow_copies(i):
        lo, hi = spans[i]
        pairs = ((east, flows_e), (north, flows_n), (mask, lands))
        return [pltpu.make_async_copy(a.at[lo:hi], b.at[lo:hi], level_sem.at[1 + j, i]) for j, (a, b) in enumerate(pairs)]

    def out_copy(i):
        lo, hi = sends[i]
        return pltpu.make_async_copy(results.at[:, lo - first : hi - first], out.at[:, lo:hi], out_sem.at[i])

    cell_copy(0).start()
    for copy in flow_copies(0) + halo_copies():
        copy.start()
    for i in range(1, len(spans)):
        cell_copy(i).start()
        for copy in flow_copies(i):
            copy.start()
    for copy in halo_copies():
        copy.wait()

    @pl.when(top[0] > 0)
    def _():
        field = lax.broadcasted_iota(jnp.int32, ghost_v.shape, 1)
        above_v[:, 0] = jnp.where(field == 7, 1.0, ghost_v[...])
        above_v[:, 1] = ghost_v[...]

    for lo in range(first, levels, EDGE_LEVELS):
        ks = range(lo, min(lo + EDGE_LEVELS, levels))
        stacked = (8 * len(ks), LANES)
        lane_of_four = lanes_of(stacked) % 4

        def stack(ref, j, h):
            return jnp.concatenate([ref[min(k + j, levels - 1), h] for k in ks], 0)

        slopes, fluxes = edge_values(
            lambda j, h: jnp.where(lane_of_four < 2, stack(west_v, j, h), stack(east_v, j, h)),
            lambda j, h: stack(own_v, j, h),
        )
        for i, k in enumerate(ks):
            edges[k, 0] = slopes[8 * i : 8 * i + 8]
            edges[k, 1] = fluxes[8 * i : 8 * i + 8]
    for copy in flow_copies(0) + [cell_copy(0)]:
        copy.wait()

    def several(i, _):
        k0 = first + i * together
        for i in range(1, len(spans)):

            @pl.when(jnp.logical_and(k0 + together >= spans[i][0], k0 < spans[i][0]))
            def _():
                for copy in flow_copies(i) + [cell_copy(i)]:
                    copy.wait()

        size = len(scratch) // together
        in_step(*[one(k0 + j, scratch[j * size : (j + 1) * size]) for j in range(together)])
        for i in range(len(sends)):

            @pl.when(k0 + together == sends[i][1])
            def _():
                out_copy(i).start()

        return 0

    def one(k, scratch):
        level = {-1: k - 1, 0: k, 1: jnp.minimum(k + 1, levels - 1)}

        def write(t, part, value):
            results[t, k - first, part] = value

        return level_step(
            cells.at[:, k - 1],
            cells.at[:, k],
            cells.at[:, level[1]],
            lambda j, i: below_v[level[j], i],
            lambda j, i: above_v[level[j], i],
            edges[k, 0],
            edges[k, 1],
            flows_e[k],
            flows_n[k],
            lands[k].astype(F32),
            write,
            scratch,
        )

    lax.fori_loop(0, (levels - first) // together, several, 0)
    for i in range(len(sends)):
        out_copy(i).wait()


def deep_levels(first, top, tracers, east, north, mask, west_cols, east_cols, own_cols, row_below, row_above, ghost):
    levels = tracers.shape[1]
    halos = (west_cols, east_cols, own_cols, row_below, row_above, ghost)
    flow = (levels, ROWS, LANES)
    return pl.pallas_call(
        functools.partial(deep_kernel, first, TOGETHER),
        in_specs=[pl.BlockSpec(memory_space=pltpu.SMEM)]
        + [pl.BlockSpec(memory_space=pltpu.HBM)] * 4
        + [pl.BlockSpec(memory_space=pl.ANY)] * 6,
        out_specs=pl.BlockSpec(memory_space=pl.ANY),
        out_shape=jax.ShapeDtypeStruct(tracers.shape, F32),
        scratch_shapes=[
            pltpu.VMEM((NTR, levels, ROWS + 16, LANES), F32),
            pltpu.VMEM(flow, F32),
            pltpu.VMEM(flow, F32),
            pltpu.VMEM(flow, jnp.int32),
        ]
        + [pltpu.VMEM(x.shape, F32) for x in halos]
        + [
            pltpu.VMEM((NTR, levels - first, ROWS, LANES), F32),
            pltpu.VMEM((levels, 2, 8, LANES), F32),
            pltpu.SemaphoreType.DMA((6,)),
            pltpu.SemaphoreType.DMA((4, levels)),
            pltpu.SemaphoreType.DMA((levels,)),
        ]
        + level_scratch() * TOGETHER,
        compiler_params=pltpu.CompilerParams(vmem_limit_bytes=VMEM_LIMIT),
        name="deep_levels",
    )(top, tracers, east, north, mask, *halos)


def expand(x, lane):
    total = x
    for f in range(2, 6):
        total = jnp.where(lane // 4 == f, roll(x, 4 * (f - 1)), total)
    return jnp.where(lane // 4 == 6, roll(x, 16), total)


def pack_rows(tiles, lane):
    packed = []
    for h in range(2):
        total = jnp.zeros((8, LANES), F32)
        for rr in range(4):
            total = jnp.where(lane // 32 == rr, roll(tiles[4 * h + rr], 32 * rr), total)
        packed.append(total)
    return packed


def force_columns(cols, force, lane):
    field = (lane % 32) // 4
    mask = spread(roll(cols, -28), lane % 32)
    tracer_change = mask * (force * jnp.where(field == 0, HEAT_SCALE, FRESH_SCALE * cols))
    return cols + jnp.where(field < 6, tracer_change, jnp.where(field == 6, STRESS_SCALE * force, 0.0))


def force_rows(rows, mask, heat, fresh, tau):
    field = lax.broadcasted_iota(jnp.int32, (8, LANES), 0)
    tracer_change = mask * jnp.where(field == 0, HEAT_SCALE * heat, FRESH_SCALE * fresh * rows)
    return rows + jnp.where(field < 6, tracer_change, jnp.where(field == 6, STRESS_SCALE * tau, 0.0))


def surface_kernel(
    top, arrived, tracers, east, north, mask, west_cols, east_cols, own_cols, row_below, arriving_above, ghost, _, forcing, out,
    row_above, cells, cell_sem, rows_b, rows_a, cols_h, cols_o, *scratch
):
    copy = pltpu.make_async_copy(tracers.at[:, 0:3], cells.at[:, :, 8:72], cell_sem)
    copy.start()
    devices = arrived.shape[0] // (4 * GROUPS)
    stride = 4 * GROUPS
    lane = lanes_of((8, LANES))
    lane_of_four = lane % 4

    def gathered(group, row):
        return arrived[pl.ds(4 * group + row, devices, stride=stride), :]

    labels = gathered(4, 0).T[LABEL_LANE : LABEL_LANE + 16]
    row_id = lax.broadcasted_iota(jnp.int32, (ROWS, devices), 0).astype(F32) + 1.0

    def pick(n):
        return (labels[n : n + 1] == row_id).astype(F32)

    def dot(a, b):
        return jnp.dot(a, b, precision=lax.Precision.HIGHEST, preferred_element_type=F32)

    flux = jnp.zeros((ROWS, 4 * LANES), F32)
    for n in range(4):
        flux += dot(pick(n), jnp.concatenate([gathered(n, f) for f in range(4)], 1))
    fields = [flux[:, LANES * f : LANES * (f + 1)] for f in range(4)]
    for f in range(4):
        forcing[f] = fields[f]
    heat, fresh, tau_x, tau_y = fields

    wide = lanes_of((devices, LANES))
    sides = [gathered(4, f) for f in range(3)]
    beside = jnp.zeros((ROWS, LANES), F32)
    for side in range(2):
        for n in range(4):
            back = -4 * n - 16 * side
            lined = jnp.where(
                wide < 4, roll(sides[0], back), jnp.where(wide < 8, roll(sides[1], back + 4), roll(sides[2], back + 8))
            )
            lined = jnp.where((wide < 12) & (wide % 4 // 2 == side), lined, 0.0)
            beside += dot(pick(4 + 4 * side + n), lined)

    over = [jnp.sum(gathered(5, f), 0, keepdims=True) for f in range(4)]
    under = [jnp.sum(gathered(6, f), 0, keepdims=True) for f in range(4)]
    tau_under = jnp.sum(gathered(4, 3), 0, keepdims=True)
    is_top = top[0] > 0
    field = lax.broadcasted_iota(jnp.int32, (8, LANES), 0)
    for k in range(3):
        row_above[k, 0] = jnp.where(is_top, jnp.where(field == 7, 1.0, ghost[k]), arriving_above[k, 0])
        row_above[k, 1] = jnp.where(is_top, ghost[k], arriving_above[k, 1])

    land = [mask[k].astype(F32) for k in range(2)]
    copy.wait()
    cells[0, 0, 8:72] = cells[0, 0, 8:72] + land[0] * (HEAT_SCALE * heat)
    for t in range(1, NTR):
        c = cells[t, 0, 8:72]
        cells[t, 0, 8:72] = c + land[0] * (FRESH_SCALE * fresh * c)
    rows_b[0] = force_rows(row_below[0, 0], row_below[0, 0, 7:8], under[2], under[3], 0.0)
    rows_b[1] = force_rows(row_below[0, 1], row_below[0, 1, 7:8], under[0], under[1], tau_under)
    near = jnp.where(is_top, row_above[0, 1, 7:8], row_above[0, 0, 7:8])
    rows_a[0] = force_rows(row_above[0, 0], near, over[0], over[1], 0.0)
    rows_a[1] = force_rows(row_above[0, 1], row_above[0, 1, 7:8], over[2], over[3], 0.0)
    own_tiles, halo_tiles = [], []
    for r in range(8):
        part = slice(8 * r, 8 * r + 8)
        mine = jnp.where(lane < 4, roll(heat[part], 2), jnp.where(lane < 8, roll(fresh[part], 6), roll(tau_x[part], 10)))
        own_tiles.append(expand(mine, lane))
        halo_tiles.append(expand(beside[part], lane))
    own_force, halo_force = pack_rows(own_tiles, lane), pack_rows(halo_tiles, lane)
    for h in range(2):
        cols = jnp.where(lane_of_four < 2, west_cols[0, h], east_cols[0, h])
        cols_h[h] = force_columns(cols, halo_force[h], lane)
        cols_o[h] = force_columns(own_cols[0, h], own_force[h], lane)

    def level(k):
        def at(j):
            return max(k + j, 0)

        def write(t, part, value):
            out[t, k, part] = value

        size = len(scratch) // 2
        return level_step(
            cells.at[:, at(-1)],
            cells.at[:, k],
            cells.at[:, k + 1],
            lambda j, i: rows_b[i] if at(j) == 0 else row_below[at(j), i],
            lambda j, i: rows_a[i] if at(j) == 0 else row_above[at(j), i],
            slopes[8 * k : 8 * k + 8],
            fluxes[8 * k : 8 * k + 8],
            east[k] + STRESS_SCALE * tau_x if k == 0 else east[k],
            north[k] + STRESS_SCALE * tau_y if k == 0 else north[k],
            land[k],
            write,
            scratch[size * k : size * (k + 1)],
        )

    def halo_at(k, h):
        return cols_h[h] if k <= 0 else jnp.where(lane_of_four < 2, west_cols[k, h], east_cols[k, h])

    def own_at(k, h):
        return cols_o[h] if k <= 0 else own_cols[k, h]

    slopes, fluxes = edge_values(
        lambda j, h: jnp.concatenate([halo_at(k + j, h) for k in range(2)], 0),
        lambda j, h: jnp.concatenate([own_at(k + j, h) for k in range(2)], 0),
    )
    in_step(level(0), level(1))


def surface_levels(top, arrived, tracers, east, north, mask, west_cols, east_cols, own_cols, row_below, row_above, ghost, done):
    block = lambda n: pl.BlockSpec((NTR, n, ROWS, LANES), lambda i: (0, 0, 0, 0))
    flow = pl.BlockSpec((2, ROWS, LANES), lambda i: (0, 0, 0))
    halo = lambda x: pl.BlockSpec((3,) + x.shape[1:], lambda i: (0,) * x.ndim)
    return pl.pallas_call(
        surface_kernel,
        grid=(1,),
        in_specs=[
            pl.BlockSpec(memory_space=pltpu.SMEM),
            pl.BlockSpec(arrived.shape, lambda i: (0, 0)),
            pl.BlockSpec(memory_space=pltpu.HBM),
            flow,
            flow,
            flow,
        ]
        + [halo(x) for x in (west_cols, east_cols, own_cols, row_below, row_above, ghost)]
        + [pl.BlockSpec(memory_space=pltpu.HBM)],
        out_specs=[pl.BlockSpec((4, ROWS, LANES), lambda i: (0, 0, 0)), block(2)],
        out_shape=[jax.ShapeDtypeStruct((4, ROWS, LANES), F32), jax.ShapeDtypeStruct(tracers.shape, F32)],
        input_output_aliases={12: 1},
        scratch_shapes=[
            pltpu.VMEM((3, 2, 8, LANES), F32),
            pltpu.VMEM((NTR, 3, ROWS + 16, LANES), F32),
            pltpu.SemaphoreType.DMA,
            pltpu.VMEM((2, 8, LANES), F32),
            pltpu.VMEM((2, 8, LANES), F32),
            pltpu.VMEM((2, 8, LANES), F32),
            pltpu.VMEM((2, 8, LANES), F32),
        ]
        + level_scratch() * 2,
        compiler_params=pltpu.CompilerParams(vmem_limit_bytes=VMEM_LIMIT),
        name="surface_levels",
    )(top, arrived, tracers, east, north, mask, west_cols, east_cols, own_cols, row_below, row_above, ghost, done)


def strip_kernel(c, own, west, out):
    low = c[0] % LANES
    levels = own.shape[0]
    lane = lanes_of((levels, 8, LANES))
    joined = jnp.where(lane <= low, own[:, 0], west[:, 0]).reshape(levels * 8, LANES)
    out[...] = reversed_lanes(joined, low).reshape(levels, 8, LANES)


def fold_strip(both, west_cols, c):
    levels = both.shape[0]
    top = pl.BlockSpec((levels, 1, 8, LANES), lambda i: (0, 2, 0, 0))
    return pl.pallas_call(
        strip_kernel,
        grid=(1,),
        in_specs=[pl.BlockSpec(memory_space=pltpu.SMEM), top, top],
        out_specs=pl.BlockSpec((levels, 8, LANES), lambda i: (0, 0, 0)),
        out_shape=jax.ShapeDtypeStruct((levels, 8, LANES), F32),
        name="fold_strip",
    )(c, both, west_cols)


def body(tracers, flow_east, flow_north, sea_mask, atm_fields, remap_weights, remap_src, remap_dst, fold_partner):
    n_lon, n_lat = lax.axis_size("lon"), lax.axis_size("lat")
    devices = n_lon * n_lat
    lon, lat = lax.axis_index("lon"), lax.axis_index("lat")
    c = (fold_partner[0] + lon * LANES) % (n_lon * LANES)
    top = (lat == n_lat - 1).astype(jnp.int32)[None]

    both, own_cols, up, down = pack_halos(tracers, flow_east, flow_north, sea_mask)
    right = [(i, (i + 1) % n_lon) for i in range(n_lon)]
    left = [(j, i) for i, j in right]
    north = [(i, i + 1) for i in range(n_lat - 1)]
    south = [(j, i) for i, j in north]
    west_cols = lax.ppermute(both, "lon", right)
    row_below = lax.ppermute(up, "lat", north)
    row_above = lax.ppermute(down, "lat", south)
    east_cols = lax.ppermute(own_cols, "lon", left)
    atm_fields, _ = lax.optimization_barrier((atm_fields, both))
    outgoing = remap(atm_fields, remap_weights, remap_src, remap_dst, c[None], n_lon, n_lat)
    west_cols, outgoing = lax.optimization_barrier((west_cols, outgoing))
    strip = fold_strip(both, west_cols, c[None])

    def move(b):
        pairs = [(q * n_lat + n_lat - 1, ((b - q) % n_lon) * n_lat + n_lat - 1) for q in range(n_lon)]
        return lambda x: lax.ppermute(x, ("lon", "lat"), pairs)

    ghost = lax.switch(c // LANES, [move(b) for b in range(n_lon)], strip)
    outgoing, ghost, east_cols, row_below, row_above = lax.optimization_barrier(
        (outgoing, ghost, east_cols, row_below, row_above)
    )
    arrived = lax.all_to_all(outgoing, ("lon", "lat"), split_axis=0, concat_axis=0, tiled=True)
    halos = (west_cols, east_cols, own_cols, row_below, row_above, ghost)
    done = deep_levels(2, top, tracers, flow_east, flow_north, sea_mask, *halos)
    arrived = arrived.reshape(devices * 4 * GROUPS, LANES)
    return surface_levels(top, arrived, tracers, flow_east, flow_north, sea_mask, *halos, done)


def solution(mesh):
    placed = (
        P(None, None, "lat", "lon"),
        P(None, "lat", "lon"),
        P(None, "lat", "lon"),
        P(None, "lat", "lon"),
        P(None, ("lon", "lat")),
        P(("lon", "lat"), None, None),
        P(("lon", "lat")),
        P(("lon", "lat")),
        P("lon"),
    )
    return jax.shard_map(
        body,
        mesh=mesh,
        in_specs=placed,
        out_specs=(P(None, "lat", "lon"), P(None, None, "lat", "lon")),
        check_vma=False,
    )
```

profile of v0, /device:TPU:0, one launch (start us, length us, event | category | flops | bytes accessed | tf_op | source)
XLA Modules:
  0.0 80.8 jit_solution(13290610751831852580)
XLA Ops:
  0.6 0.0 copy-start.5
  0.6 4.6 %pack_halos.1 = (f32[24,3,8,128]{3,2,1,0:T(8,128)}, f32[24,2,8,128]{3,2,1,0:T(8,128)}, f32[24,2,8,128]{3,2,1,0:T(8,128)}, f32[24,2,8,128]{3,2,1,0:T(8,128)}) custom-call(f32[6,24,64,128]{3,2,1,0:T(8,128)} %tracers.5, f32[24,64,128]{2,1,0:T(8,128)} %east.5, f32[24,64,128]{2,1,0:T(8,128)} %north.5, s32[24,64,128]{2,1,0:T(8,128)} %mask.5), custom_call_target="tpu_custom_call" | custom-call | tf_op jit(solution)/shard_map/pack_halos/pallas_call | solution.py:109
  5.3 0.1 collective-permute-start.16
  5.3 3.9 %collective-permute-start.18 = (f32[24,2,8,128]{3,2,1,0:T(8,128)}, f32[24,2,8,128]{3,2,1,0:T(8,128)S(1)}, u32[]{:S(2)}, u32[]{:S(2)}) collective-permute-start(f32[24,2,8,128]{3,2,1,0:T(8,128)} %get-tuple-element.52), channel_id=1, source_target_pairs={{0,1},{1,2},{2,3},{3,4},{4,5},{5,6},{6,7},{8,9},{9,10},{10,11},{11... | collective-permute-start | bytes 589832 | tf_op jit(solution)/shard_map/ppermute | solution.py:797
  9.3 1.3 %collective-permute-start.19 = (f32[24,2,8,128]{3,2,1,0:T(8,128)}, f32[24,2,8,128]{3,2,1,0:T(8,128)S(1)}, u32[]{:S(2)}, u32[]{:S(2)}) collective-permute-start(f32[24,2,8,128]{3,2,1,0:T(8,128)} %get-tuple-element.53), channel_id=1, source_target_pairs={{1,0},{2,1},{3,2},{4,3},{5,4},{6,5},{7,6},{9,8},{10,9},{11,10},{12... | collective-permute-start | bytes 589832 | tf_op jit(solution)/shard_map/ppermute | solution.py:798
  10.6 5.1 %collective-permute-start.17 = (f32[24,2,8,128]{3,2,1,0:T(8,128)}, f32[24,2,8,128]{3,2,1,0:T(8,128)S(1)}, u32[]{:S(2)}, u32[]{:S(2)}) collective-permute-start(f32[24,2,8,128]{3,2,1,0:T(8,128)} %get-tuple-element.51.own_cols), channel_id=1, source_target_pairs={{8,0},{16,8},{24,16},{32,24},{40,32},{48,40},{56,48},{64,56},{72,6... | collective-permute-start | bytes 589832 | tf_op jit(solution)/shard_map/ppermute | solution.py:799
  15.7 0.0 copy-done.5
  15.8 10.4 %remap.1 = f32[896,4,128]{2,1,0:T(4,128)} custom-call(s32[256]{0:T(256)} %src.1, s32[256]{0:T(256)} %dst.1, s32[1]{0:T(128)} %bitcast.2.fold.c, bf16[4,8192]{1,0:T(4,128)(2,1)} %atm, bf16[256,128,128]{2,1,0:T(8,128)(2,1)} %weights_hbm.1), custom_call_target="tpu_custom_call" | custom-call | tf_op jit(solution)/shard_map/remap/pallas_call | solution.py:246
  26.1 0.0 collective-permute-done.16.west.west_cols
  26.2 0.0 copy-start.1
  26.2 0.7 copy-done.1
  26.9 1.2 %fold_strip.1 = f32[24,8,128]{2,1,0:T(8,128)S(1)} custom-call(s32[1]{0:T(128)} %bitcast.2.fold.c, f32[24,3,8,128]{3,2,1,0:T(8,128)} %get-tuple-element.47.own, f32[24,3,8,128]{3,2,1,0:T(8,128)} %copy-done.1), custom_call_target="tpu_custom_call" | custom-call | tf_op jit(solution)/shard_map/fold_strip/pallas_call | solution.py:774
  28.1 1.3 %conditional.1 = (f32[24,8,128]{2,1,0:T(8,128)}) conditional(s32[]{:T(128)} %clamp.3, f32[24,8,128]{2,1,0:T(8,128)S(1)} %fold_strip.1, f32[24,8,128]{2,1,0:T(8,128)S(1)} %fold_strip.1, f32[24,8,128]{2,1,0:T(8,128)S(1)} %fold_strip.1, f32[24,8,128]{2,1,0:T(8,128)S(1)} %fold_strip.1, ...), branch_computations={%region_0.1_spmd, %region_1.2_spmd, %region_2.3_spmd, %region_3.4_... | conditional | bytes 393264 | solution.py:809
  28.1 1.3 %collective-permute-start.15 = (f32[24,8,128]{2,1,0:T(8,128)S(1)}, f32[24,8,128]{2,1,0:T(8,128)}, u32[]{:S(2)}, u32[]{:S(2)}) collective-permute-start(f32[24,8,128]{2,1,0:T(8,128)S(1)} %param.15), channel_id=1, source_target_pairs={{7,127},{15,119},{23,111},{31,103},{39,95},{47,87},{55,79},{63,71}... | collective-permute-start | bytes 294920 | tf_op jit(solution)/shard_map/cond/branch_15_fun/ppermute | solution.py:807
  29.4 0.0 collective-permute-done.15
  29.4 0.0 collective-permute-done.18.row_below
  29.4 0.0 collective-permute-done.19.row_above.arriving_above
  29.4 0.0 copy-start.3
  29.4 0.0 collective-permute-done.17.east_cols
  29.5 17.3 %all-to-all-start = ((f32[896,4,128]{2,1,0:T(4,128)}), f32[896,4,128]{2,1,0:T(4,128)S(1)}, u32[]{:S(2)}, u32[]{:S(2)}) async-start(f32[896,4,128]{2,1,0:T(4,128)} %remap.1), calls=%async_computation | async-start | bytes 3670016 | tf_op jit(solution)/shard_map/all_to_all | solution.py:813
  46.8 16.3 %deep_levels.1._ = f32[6,24,64,128]{3,2,1,0:T(8,128)} custom-call(s32[1]{0:T(128)} %bitcast.top, f32[6,24,64,128]{3,2,1,0:T(8,128)} %tracers.5, f32[24,64,128]{2,1,0:T(8,128)} %east.5, f32[24,64,128]{2,1,0:T(8,128)} %north.5, s32[24,64,128]{2,1,0:T(8,128)} %mask.5, f32[24,3,8,128]{3,2,1,0:T(8,128)} %copy-done.1, f32[24,2,8,128]{3,2,1,0:T(8,128)} %copy-done.4, ...), custom_call_target="tpu_custom_call" | custom-call | tf_op jit(solution)/shard_map/deep_levels/pallas_call | solution.py:560
  63.1 11.2 %all-to-all-done = f32[896,4,128]{2,1,0:T(4,128)S(1)} async-done(((f32[896,4,128]{2,1,0:T(4,128)}), f32[896,4,128]{2,1,0:T(4,128)S(1)}, u32[]{:S(2)}, u32[]{:S(2)}) %all-to-all-start) | async-done | bytes 1835040 | tf_op jit(solution)/shard_map/all_to_all | solution.py:813
  74.3 1.2 %copy-done = f32[896,4,128]{2,1,0:T(4,128)} copy-done((f32[896,4,128]{2,1,0:T(4,128)}, f32[896,4,128]{2,1,0:T(4,128)S(1)}, u32[]{:S(2)}) %copy-start) | copy-done | bytes 1835032
  75.6 5.2 %surface_levels.1 = (f32[4,64,128]{2,1,0:T(8,128)}, f32[6,24,64,128]{3,2,1,0:T(8,128)}) custom-call(s32[1]{0:T(128)} %bitcast.top, f32[3584,128]{1,0:T(8,128)} %bitcast.5, f32[6,24,64,128]{3,2,1,0:T(8,128)} %tracers.5, f32[24,64,128]{2,1,0:T(8,128)} %east.5, f32[24,64,128]{2,1,0:T(8,128)} %north.5, ...), custom_call_target="tpu_custom_call", output_to_operand_aliasing={{1}: (12, {})} | custom-call | tf_op jit(solution)/shard_map/surface_levels/pallas_call | solution.py:732
  (6 shorter events, 0.0 us)
Async XLA Ops:
  0.6 15.1 %copy-start.5 = (s32[128]{0:T(128)S(1)}, s32[128]{0:T(128)}, u32[]{:S(2)}) copy-start(s32[128]{0:T(128)} %param.33) | copy-start | bytes 1540
  5.3 20.9 %collective-permute-start.16 = (f32[24,3,8,128]{3,2,1,0:T(8,128)}, f32[24,3,8,128]{3,2,1,0:T(8,128)S(1)}, u32[]{:S(2)}, u32[]{:S(2)}) collective-permute-start(f32[24,3,8,128]{3,2,1,0:T(8,128)} %get-tuple-element.47.own), channel_id=1, source_target_pairs={{0,8},{8,16},{16,24},{24,32},{32,40},{40,48},{48,56},{56,64},{64,7... | collective-permute-start | bytes 884744 | tf_op jit(solution)/shard_map/ppermute | solution.py:796
  5.3 24.1 %collective-permute-start.18 = (f32[24,2,8,128]{3,2,1,0:T(8,128)}, f32[24,2,8,128]{3,2,1,0:T(8,128)S(1)}, u32[]{:S(2)}, u32[]{:S(2)}) collective-permute-start(f32[24,2,8,128]{3,2,1,0:T(8,128)} %get-tuple-element.52), channel_id=1, source_target_pairs={{0,1},{1,2},{2,3},{3,4},{4,5},{5,6},{6,7},{8,9},{9,10},{10,11},{11... | collective-permute-start | bytes 589832 | tf_op jit(solution)/shard_map/ppermute | solution.py:797
  9.3 20.1 %collective-permute-start.19 = (f32[24,2,8,128]{3,2,1,0:T(8,128)}, f32[24,2,8,128]{3,2,1,0:T(8,128)S(1)}, u32[]{:S(2)}, u32[]{:S(2)}) collective-permute-start(f32[24,2,8,128]{3,2,1,0:T(8,128)} %get-tuple-element.53), channel_id=1, source_target_pairs={{1,0},{2,1},{3,2},{4,3},{5,4},{6,5},{7,6},{9,8},{10,9},{11,10},{12... | collective-permute-start | bytes 589832 | tf_op jit(solution)/shard_map/ppermute | solution.py:798
  10.6 18.9 %collective-permute-start.17 = (f32[24,2,8,128]{3,2,1,0:T(8,128)}, f32[24,2,8,128]{3,2,1,0:T(8,128)S(1)}, u32[]{:S(2)}, u32[]{:S(2)}) collective-permute-start(f32[24,2,8,128]{3,2,1,0:T(8,128)} %get-tuple-element.51.own_cols), channel_id=1, source_target_pairs={{8,0},{16,8},{24,16},{32,24},{40,32},{48,40},{56,48},{64,56},{72,6... | collective-permute-start | bytes 589832 | tf_op jit(solution)/shard_map/ppermute | solution.py:799
  26.2 0.7 copy-start.1
  28.1 1.3 %collective-permute-start.15 = (f32[24,8,128]{2,1,0:T(8,128)S(1)}, f32[24,8,128]{2,1,0:T(8,128)}, u32[]{:S(2)}, u32[]{:S(2)}) collective-permute-start(f32[24,8,128]{2,1,0:T(8,128)S(1)} %param.15), channel_id=1, source_target_pairs={{7,127},{15,119},{23,111},{31,103},{39,95},{47,87},{55,79},{63,71}... | collective-permute-start | bytes 294920 | tf_op jit(solution)/shard_map/cond/branch_15_fun/ppermute | solution.py:807
  29.4 17.4 %copy-start.2 = (f32[24,2,8,128]{3,2,1,0:T(8,128)}, f32[24,2,8,128]{3,2,1,0:T(8,128)S(1)}, u32[]{:S(2)}) copy-start(f32[24,2,8,128]{3,2,1,0:T(8,128)S(1)} %collective-permute-done.18.row_below) | copy-start | bytes 589828
  29.4 17.4 %copy-start.3 = (f32[24,2,8,128]{3,2,1,0:T(8,128)}, f32[24,2,8,128]{3,2,1,0:T(8,128)S(1)}, u32[]{:S(2)}) copy-start(f32[24,2,8,128]{3,2,1,0:T(8,128)S(1)} %collective-permute-done.19.row_above.arriving_above) | copy-start | bytes 589828
  29.4 17.3 %copy-start.4 = (f32[24,2,8,128]{3,2,1,0:T(8,128)}, f32[24,2,8,128]{3,2,1,0:T(8,128)S(1)}, u32[]{:S(2)}) copy-start(f32[24,2,8,128]{3,2,1,0:T(8,128)S(1)} %collective-permute-done.17.east_cols) | copy-start | bytes 589828
  29.5 44.9 %all-to-all-start = ((f32[896,4,128]{2,1,0:T(4,128)}), f32[896,4,128]{2,1,0:T(4,128)S(1)}, u32[]{:S(2)}, u32[]{:S(2)}) async-start(f32[896,4,128]{2,1,0:T(4,128)} %remap.1), calls=%async_computation | async-start | bytes 3670016 | tf_op jit(solution)/shard_map/all_to_all | solution.py:813
  74.3 1.2 %copy-start = (f32[896,4,128]{2,1,0:T(4,128)}, f32[896,4,128]{2,1,0:T(4,128)S(1)}, u32[]{:S(2)}) copy-start(f32[896,4,128]{2,1,0:T(4,128)S(1)} %all-to-all-done) | copy-start | bytes 5505028
where the time goes:
time: 81.3 us; the launch traced here: 80.8 us
  Pallas kernels  37.7 us (46%)
  starting transfers between devices  29 us (36%)
  waiting for transfers between devices  11.2 us (14%)
  local copies, waits for them, and re-layouts  1.97 us (2%)
  between operations  0.87 us (1%)
    all_to_all x1, starting transfers between devices, body(): lax.all_to_all(outgoing, ('lon', 'lat'), split_axis=0, concat_axis=0, til...  17.3 us
    pallas_call x1, Pallas kernels, deep_levels(): pl.pallas_call(functools.partial(deep_kernel, first, TOGETHER), in_specs=...  16.3 us
    all_to_all x1, waiting for transfers between devices, body(): lax.all_to_all(outgoing, ('lon', 'lat'), split_axis=0, concat_axis=0, til...  11.2 us
    pallas_call x1, Pallas kernels, remap(): pl.pallas_call(functools.partial(remap_kernel, n_lon, n_lat), in_specs=[s...  10.4 us
    pallas_call x1, Pallas kernels, surface_levels(): pl.pallas_call(surface_kernel, grid=(1,), in_specs=[pl.BlockSpec(memory_s...  5.24 us
    ppermute x1, starting transfers between devices, body(): east_cols = lax.ppermute(own_cols, 'lon', left)  5.12 us
    pallas_call x1, Pallas kernels, pack_halos(): pl.pallas_call(pack_kernel, in_specs=[pl.BlockSpec(memory_space=pltpu.HBM...  4.61 us
    ppermute x1, starting transfers between devices, body(): row_below = lax.ppermute(up, 'lat', north)  3.92 us
  transfers between devices with their start and end apart: 6, of which 1 were waited for; matrix products, arithmetic and copies ran while one was open for 0% of the time, Pallas kernels for 35%

commit v1 on v0

--- a/solution.py
+++ b/solution.py
@@ -124,6 +124,11 @@
     )(tracers, east, north, mask)
 
 
+def parts_of(x, size):
+    assert size & (size - 1) == 0
+    return lax.shift_right_logical(x, size.bit_length() - 1), x & (size - 1)
+
+
 def remap_kernel(n_lon, n_lat, src, dst, fold, atm, weights_hbm, out, weights, blocks, edge, labels, count, weight_sem):
     devices = n_lon * n_lat
     sends = weights.shape[0]
@@ -164,15 +169,13 @@
         for j in range(batch):
             w = batch * i + j
             place = dst[w]
-            lon = place & (n_lon - 1) if n_lon & (n_lon - 1) == 0 else place % n_lon
-            row = place // n_lon
-            local = row % ROWS
-            owner = lon * n_lat + row // ROWS
+            row, lon = parts_of(place, n_lon)
+            lat, local = parts_of(row, ROWS)
+            owner = lon * n_lat + lat
             slot = count[owner]
             count[owner] = slot + 1
-            kind = jnp.where(local < 2, local, local - (ROWS - 4))
-            is_edge = jnp.logical_or(local < 2, local >= ROWS - 2)
-            places.append((owner, slot, local, jnp.where(is_edge, owner * 4 + kind, devices * 4)))
+            is_edge = ((local + 2) & (ROWS - 1)) < 4
+            places.append((owner, slot, local, jnp.where(is_edge, owner * 4 + (local & 3), devices * 4)))
             lefts.append(blocks[src[w], 0:4])
         left = jnp.concatenate(lefts, 0).astype(jnp.bfloat16)
         right = weights[pl.ds(pl.multiple_of(batch * i, batch), batch)].reshape(batch * LANES, LANES)

time: 81.3 us -> 79.1 us (0.973)
  Pallas kernels: 37.7 us -> 36.1 us
  starting transfers between devices: 29 us -> 27.9 us
    pallas_call x1, Pallas kernels: 10.4 us -> 8.72 us  [remap(): pl.pallas_call(functools.partial(remap_kernel, n_lon, n_lat), in_specs=[s...]
    all_to_all x1, starting transfers between devices: 17.3 us -> 16.2 us  [body(): lax.all_to_all(outgoing, ('lon', 'lat'), split_axis=0, concat_axis=0, til...]
  transfers between devices with their start and end apart: 6 -> 6, of which waited for: 1 -> 1; matrix products, arithmetic and copies ran while one was open for 0% -> 0% of each run, Pallas kernels for 35% -> 34%
where the time goes in v1:
time: 79.1 us; the launch traced here: 78 us
  Pallas kernels  36.1 us (46%)
  starting transfers between devices  27.9 us (35%)
  waiting for transfers between devices  11.2 us (14%)
  local copies, waits for them, and re-layouts  1.97 us (2%)
  between operations  0.87 us (1%)
    pallas_call x1, Pallas kernels, deep_levels(): pl.pallas_call(functools.partial(deep_kernel, first, TOGETHER), in_specs=...  16.3 us
    all_to_all x1, starting transfers between devices, body(): lax.all_to_all(outgoing, ('lon', 'lat'), split_axis=0, concat_axis=0, til...  16.2 us
    all_to_all x1, waiting for transfers between devices, body(): lax.all_to_all(outgoing, ('lon', 'lat'), split_axis=0, concat_axis=0, til...  11.2 us
    pallas_call x1, Pallas kernels, remap(): pl.pallas_call(functools.partial(remap_kernel, n_lon, n_lat), in_specs=[s...  8.72 us
    pallas_call x1, Pallas kernels, surface_levels(): pl.pallas_call(surface_kernel, grid=(1,), in_specs=[pl.BlockSpec(memory_s...  5.24 us
    ppermute x1, starting transfers between devices, body(): east_cols = lax.ppermute(own_cols, 'lon', left)  5.12 us
    pallas_call x1, Pallas kernels, pack_halos(): pl.pallas_call(pack_kernel, in_specs=[pl.BlockSpec(memory_space=pltpu.HBM...  4.61 us
    ppermute x1, starting transfers between devices, body(): row_below = lax.ppermute(up, 'lat', north)  3.92 us
  transfers between devices with their start and end apart: 6, of which 1 were waited for; matrix products, arithmetic and copies ran while one was open for 0% of the time, Pallas kernels for 34%

profile of v1, /device:TPU:0, one launch (start us, length us, event | category | flops | bytes accessed | tf_op | source)
XLA Modules:
  0.0 78.0 jit_solution(11911291723091626785)
XLA Ops:
  0.6 0.0 copy-start.5
  0.6 4.6 %pack_halos.1 = (f32[24,3,8,128]{3,2,1,0:T(8,128)}, f32[24,2,8,128]{3,2,1,0:T(8,128)}, f32[24,2,8,128]{3,2,1,0:T(8,128)}, f32[24,2,8,128]{3,2,1,0:T(8,128)}) custom-call(f32[6,24,64,128]{3,2,1,0:T(8,128)} %tracers.5, f32[24,64,128]{2,1,0:T(8,128)} %east.5, f32[24,64,128]{2,1,0:T(8,128)} %north.5, s32[24,64,128]{2,1,0:T(8,128)} %mask.5), custom_call_target="tpu_custom_call" | custom-call | tf_op jit(solution)/shard_map/pack_halos/pallas_call | solution.py:109
  5.3 0.1 collective-permute-start.16
  5.3 3.9 %collective-permute-start.18 = (f32[24,2,8,128]{3,2,1,0:T(8,128)}, f32[24,2,8,128]{3,2,1,0:T(8,128)S(1)}, u32[]{:S(2)}, u32[]{:S(2)}) collective-permute-start(f32[24,2,8,128]{3,2,1,0:T(8,128)} %get-tuple-element.52), channel_id=1, source_target_pairs={{0,1},{1,2},{2,3},{3,4},{4,5},{5,6},{6,7},{8,9},{9,10},{10,11},{11... | collective-permute-start | bytes 589832 | tf_op jit(solution)/shard_map/ppermute | solution.py:800
  9.3 1.3 %collective-permute-start.19 = (f32[24,2,8,128]{3,2,1,0:T(8,128)}, f32[24,2,8,128]{3,2,1,0:T(8,128)S(1)}, u32[]{:S(2)}, u32[]{:S(2)}) collective-permute-start(f32[24,2,8,128]{3,2,1,0:T(8,128)} %get-tuple-element.53), channel_id=1, source_target_pairs={{1,0},{2,1},{3,2},{4,3},{5,4},{6,5},{7,6},{9,8},{10,9},{11,10},{12... | collective-permute-start | bytes 589832 | tf_op jit(solution)/shard_map/ppermute | solution.py:801
  10.6 5.1 %collective-permute-start.17 = (f32[24,2,8,128]{3,2,1,0:T(8,128)}, f32[24,2,8,128]{3,2,1,0:T(8,128)S(1)}, u32[]{:S(2)}, u32[]{:S(2)}) collective-permute-start(f32[24,2,8,128]{3,2,1,0:T(8,128)} %get-tuple-element.51.own_cols), channel_id=1, source_target_pairs={{8,0},{16,8},{24,16},{32,24},{40,32},{48,40},{56,48},{64,56},{72,6... | collective-permute-start | bytes 589832 | tf_op jit(solution)/shard_map/ppermute | solution.py:802
  15.7 0.0 copy-done.5
  15.8 8.7 %remap.1 = f32[896,4,128]{2,1,0:T(4,128)} custom-call(s32[256]{0:T(256)} %src.1, s32[256]{0:T(256)} %dst.1, s32[1]{0:T(128)} %bitcast.2.fold.c, bf16[4,8192]{1,0:T(4,128)(2,1)} %atm, bf16[256,128,128]{2,1,0:T(8,128)(2,1)} %weights_hbm.1), custom_call_target="tpu_custom_call" | custom-call | tf_op jit(solution)/shard_map/remap/pallas_call | solution.py:249
  24.5 0.0 collective-permute-done.16.west.west_cols
  24.5 0.0 copy-start.1
  24.5 0.7 copy-done.1
  25.2 1.2 %fold_strip.1 = f32[24,8,128]{2,1,0:T(8,128)S(1)} custom-call(s32[1]{0:T(128)} %bitcast.2.fold.c, f32[24,3,8,128]{3,2,1,0:T(8,128)} %get-tuple-element.47.own, f32[24,3,8,128]{3,2,1,0:T(8,128)} %copy-done.1), custom_call_target="tpu_custom_call" | custom-call | tf_op jit(solution)/shard_map/fold_strip/pallas_call | solution.py:777
  26.4 1.3 %conditional.1 = (f32[24,8,128]{2,1,0:T(8,128)}) conditional(s32[]{:T(128)} %clamp.3, f32[24,8,128]{2,1,0:T(8,128)S(1)} %fold_strip.1, f32[24,8,128]{2,1,0:T(8,128)S(1)} %fold_strip.1, f32[24,8,128]{2,1,0:T(8,128)S(1)} %fold_strip.1, f32[24,8,128]{2,1,0:T(8,128)S(1)} %fold_strip.1, ...), branch_computations={%region_0.1_spmd, %region_1.2_spmd, %region_2.3_spmd, %region_3.4_... | conditional | bytes 393264 | solution.py:812
  26.4 1.3 %collective-permute-start.4 = (f32[24,8,128]{2,1,0:T(8,128)S(1)}, f32[24,8,128]{2,1,0:T(8,128)}, u32[]{:S(2)}, u32[]{:S(2)}) collective-permute-start(f32[24,8,128]{2,1,0:T(8,128)S(1)} %param.4), channel_id=1, source_target_pairs={{7,39},{15,31},{23,23},{31,15},{39,7},{47,127},{55,119},{63,111},{... | collective-permute-start | bytes 294920 | tf_op jit(solution)/shard_map/cond/branch_4_fun/ppermute | solution.py:810
  27.7 0.0 collective-permute-done.4
  27.8 0.0 collective-permute-done.18.row_below
  27.8 0.0 collective-permute-done.19.row_above.arriving_above
  27.8 0.0 collective-permute-done.17.east_cols
  27.8 0.0 copy-start.4
  27.8 16.2 %all-to-all-start = ((f32[896,4,128]{2,1,0:T(4,128)}), f32[896,4,128]{2,1,0:T(4,128)S(1)}, u32[]{:S(2)}, u32[]{:S(2)}) async-start(f32[896,4,128]{2,1,0:T(4,128)} %remap.1), calls=%async_computation | async-start | bytes 3670016 | tf_op jit(solution)/shard_map/all_to_all | solution.py:816
  44.0 16.3 %deep_levels.1._ = f32[6,24,64,128]{3,2,1,0:T(8,128)} custom-call(s32[1]{0:T(128)} %bitcast.top, f32[6,24,64,128]{3,2,1,0:T(8,128)} %tracers.5, f32[24,64,128]{2,1,0:T(8,128)} %east.5, f32[24,64,128]{2,1,0:T(8,128)} %north.5, s32[24,64,128]{2,1,0:T(8,128)} %mask.5, f32[24,3,8,128]{3,2,1,0:T(8,128)} %copy-done.1, f32[24,2,8,128]{3,2,1,0:T(8,128)} %copy-done.4, ...), custom_call_target="tpu_custom_call" | custom-call | tf_op jit(solution)/shard_map/deep_levels/pallas_call | solution.py:563
  60.4 11.2 %all-to-all-done = f32[896,4,128]{2,1,0:T(4,128)S(1)} async-done(((f32[896,4,128]{2,1,0:T(4,128)}), f32[896,4,128]{2,1,0:T(4,128)S(1)}, u32[]{:S(2)}, u32[]{:S(2)}) %all-to-all-start) | async-done | bytes 1835040 | tf_op jit(solution)/shard_map/all_to_all | solution.py:816
  71.6 1.2 %copy-done = f32[896,4,128]{2,1,0:T(4,128)} copy-done((f32[896,4,128]{2,1,0:T(4,128)}, f32[896,4,128]{2,1,0:T(4,128)S(1)}, u32[]{:S(2)}) %copy-start) | copy-done | bytes 1835032
  72.8 5.2 %surface_levels.1 = (f32[4,64,128]{2,1,0:T(8,128)}, f32[6,24,64,128]{3,2,1,0:T(8,128)}) custom-call(s32[1]{0:T(128)} %bitcast.top, f32[3584,128]{1,0:T(8,128)} %bitcast.5, f32[6,24,64,128]{3,2,1,0:T(8,128)} %tracers.5, f32[24,64,128]{2,1,0:T(8,128)} %east.5, f32[24,64,128]{2,1,0:T(8,128)} %north.5, ...), custom_call_target="tpu_custom_call", output_to_operand_aliasing={{1}: (12, {})} | custom-call | tf_op jit(solution)/shard_map/surface_levels/pallas_call | solution.py:735
  (6 shorter events, 0.0 us)
Async XLA Ops:
  0.6 15.1 %copy-start.5 = (s32[128]{0:T(128)S(1)}, s32[128]{0:T(128)}, u32[]{:S(2)}) copy-start(s32[128]{0:T(128)} %param.33) | copy-start | bytes 1540
  5.3 19.2 %collective-permute-start.16 = (f32[24,3,8,128]{3,2,1,0:T(8,128)}, f32[24,3,8,128]{3,2,1,0:T(8,128)S(1)}, u32[]{:S(2)}, u32[]{:S(2)}) collective-permute-start(f32[24,3,8,128]{3,2,1,0:T(8,128)} %get-tuple-element.47.own), channel_id=1, source_target_pairs={{0,8},{8,16},{16,24},{24,32},{32,40},{40,48},{48,56},{56,64},{64,7... | collective-permute-start | bytes 884744 | tf_op jit(solution)/shard_map/ppermute | solution.py:799
  5.3 22.4 %collective-permute-start.18 = (f32[24,2,8,128]{3,2,1,0:T(8,128)}, f32[24,2,8,128]{3,2,1,0:T(8,128)S(1)}, u32[]{:S(2)}, u32[]{:S(2)}) collective-permute-start(f32[24,2,8,128]{3,2,1,0:T(8,128)} %get-tuple-element.52), channel_id=1, source_target_pairs={{0,1},{1,2},{2,3},{3,4},{4,5},{5,6},{6,7},{8,9},{9,10},{10,11},{11... | collective-permute-start | bytes 589832 | tf_op jit(solution)/shard_map/ppermute | solution.py:800
  9.3 18.5 %collective-permute-start.19 = (f32[24,2,8,128]{3,2,1,0:T(8,128)}, f32[24,2,8,128]{3,2,1,0:T(8,128)S(1)}, u32[]{:S(2)}, u32[]{:S(2)}) collective-permute-start(f32[24,2,8,128]{3,2,1,0:T(8,128)} %get-tuple-element.53), channel_id=1, source_target_pairs={{1,0},{2,1},{3,2},{4,3},{5,4},{6,5},{7,6},{9,8},{10,9},{11,10},{12... | collective-permute-start | bytes 589832 | tf_op jit(solution)/shard_map/ppermute | solution.py:801
  10.6 17.2 %collective-permute-start.17 = (f32[24,2,8,128]{3,2,1,0:T(8,128)}, f32[24,2,8,128]{3,2,1,0:T(8,128)S(1)}, u32[]{:S(2)}, u32[]{:S(2)}) collective-permute-start(f32[24,2,8,128]{3,2,1,0:T(8,128)} %get-tuple-element.51.own_cols), channel_id=1, source_target_pairs={{8,0},{16,8},{24,16},{32,24},{40,32},{48,40},{56,48},{64,56},{72,6... | collective-permute-start | bytes 589832 | tf_op jit(solution)/shard_map/ppermute | solution.py:802
  24.5 0.7 copy-start.1
  26.4 1.3 %collective-permute-start.4 = (f32[24,8,128]{2,1,0:T(8,128)S(1)}, f32[24,8,128]{2,1,0:T(8,128)}, u32[]{:S(2)}, u32[]{:S(2)}) collective-permute-start(f32[24,8,128]{2,1,0:T(8,128)S(1)} %param.4), channel_id=1, source_target_pairs={{7,39},{15,31},{23,23},{31,15},{39,7},{47,127},{55,119},{63,111},{... | collective-permute-start | bytes 294920 | tf_op jit(solution)/shard_map/cond/branch_4_fun/ppermute | solution.py:810
  27.8 16.3 %copy-start.2 = (f32[24,2,8,128]{3,2,1,0:T(8,128)}, f32[24,2,8,128]{3,2,1,0:T(8,128)S(1)}, u32[]{:S(2)}) copy-start(f32[24,2,8,128]{3,2,1,0:T(8,128)S(1)} %collective-permute-done.18.row_below) | copy-start | bytes 589828
  27.8 16.2 %copy-start.3 = (f32[24,2,8,128]{3,2,1,0:T(8,128)}, f32[24,2,8,128]{3,2,1,0:T(8,128)S(1)}, u32[]{:S(2)}) copy-start(f32[24,2,8,128]{3,2,1,0:T(8,128)S(1)} %collective-permute-done.19.row_above.arriving_above) | copy-start | bytes 589828
  27.8 16.2 %copy-start.4 = (f32[24,2,8,128]{3,2,1,0:T(8,128)}, f32[24,2,8,128]{3,2,1,0:T(8,128)S(1)}, u32[]{:S(2)}) copy-start(f32[24,2,8,128]{3,2,1,0:T(8,128)S(1)} %collective-permute-done.17.east_cols) | copy-start | bytes 589828
  27.8 43.7 %all-to-all-start = ((f32[896,4,128]{2,1,0:T(4,128)}), f32[896,4,128]{2,1,0:T(4,128)S(1)}, u32[]{:S(2)}, u32[]{:S(2)}) async-start(f32[896,4,128]{2,1,0:T(4,128)} %remap.1), calls=%async_computation | async-start | bytes 3670016 | tf_op jit(solution)/shard_map/all_to_all | solution.py:816
  71.6 1.2 %copy-start = (f32[896,4,128]{2,1,0:T(4,128)}, f32[896,4,128]{2,1,0:T(4,128)S(1)}, u32[]{:S(2)}) copy-start(f32[896,4,128]{2,1,0:T(4,128)S(1)} %all-to-all-done) | copy-start | bytes 5505028
